TPU v7x, 256 devices: a whole 4x4x8 slice. The times are simulated.
256 devices in a mesh: space: 8 (over x, y_lo), snap: 32 (over y_hi, z, core).
Axes of the slice: x: 4, y: 4 (y_hi: 2, y_lo: 2; y = y_hi * 2 + y_lo), z: 8, core: 2. Of those that a mesh axis runs over, the one named last changes fastest.
Arguments:
- snapshots: bfloat16 [8192, 131072], P('space', 'snap'), may hold values from -6 to 6
- vectors_cyclic: float32 [131072, 64], P('snap', 'space'), may hold values from -0.015625 to 0.015625
- eigen_values: float32 [64], replicated, may hold values from 0.25 to 25
- held_out: bfloat16 [8192, 256], P(('space', 'snap')), may hold values from -6 to 6
Outputs:
- modes: bfloat16 [8192, 64], P(('space', 'snap'))
- coefficients: float32 [64, 256], replicated
All inputs are finite; a program needn't handle non-finite values.
Results may differ from a plain program's by a relative error of at most 0.0052.
Values sent between devices are 32-bit elements; how exact they have to be, the bound alone decides.
A program may use at most 64 MiB of HBM per device.

v0:
```python
import math

import jax
import jax.numpy as jnp
from jax import lax
from jax.sharding import PartitionSpec as P

ROW_BLOCK = 16
COL_BLOCK = 4


def order_rows(received, snap_count):
    slab_rows, width = received.shape
    blocks_each = slab_rows // (snap_count * ROW_BLOCK)
    shaped = received.reshape(snap_count, blocks_each, ROW_BLOCK, width)
    return shaped.transpose(1, 0, 2, 3).reshape(slab_rows, width)


def order_columns(gathered, space_count):
    slab_rows, width = gathered.shape
    shaped = gathered.reshape(slab_rows, space_count, width // (space_count * COL_BLOCK), COL_BLOCK)
    return shaped.transpose(0, 2, 1, 3).reshape(slab_rows, width)


def per_device(snapshots, vectors_cyclic, eigen_values, held_out):
    snap_count = lax.axis_size("snap")
    space_count = lax.axis_size("space")
    widened = lax.all_gather(vectors_cyclic, "space", axis=1, tiled=True)
    widened = order_columns(widened, space_count)
    moved = lax.all_to_all(widened, "snap", split_axis=0, concat_axis=0, tiled=True)
    eigvec = order_rows(moved, snap_count)
    scaled = (eigvec * lax.rsqrt(eigen_values)[None, :]).astype(jnp.bfloat16)
    summed = lax.psum_scatter(
        jnp.dot(snapshots, scaled, preferred_element_type=jnp.float32),
        "snap",
        scatter_dimension=0,
        tiled=True,
    )
    modes = summed.astype(jnp.bfloat16)
    total_cells = snapshots.shape[0] * space_count
    partial_value = lax.dot_general(
        modes, held_out, (((0,), (0,)), ((), ())), preferred_element_type=jnp.float32
    )
    coefficients = lax.psum(partial_value, ("space", "snap")) / math.sqrt(total_cells)
    return (modes, coefficients)


def solution(mesh):
    return jax.shard_map(
        per_device,
        mesh=mesh,
        in_specs=(P("space", "snap"), P("snap", "space"), P(), P(("space", "snap"), None)),
        out_specs=(P(("space", "snap"), None), P()),
        check_vma=False,
    )
```

profile of v0, /device:TPU:1, one launch (start us, length us, event | category | flops | bytes accessed | tf_op | source)
XLA Modules:
  0.0 466.0 jit_solution(14016027421047598528)
XLA Ops:
  7.2 0.0 copy-start
  7.2 0.0 all-gather.2.cloned.1.call-start
  7.2 0.7 all-gather.2.cloned.1.call-update
  7.9 42.8 %all-gather.2.cloned.1.call-done = f32[4096,64]{0,1:T(8,128)} async-done(((f32[4096,8]{0,1:T(8,128)}), f32[4096,64]{0,1:T(8,128)}) %all-gather.2.cloned.1.call-update) | async-done | bytes 1048592 | tf_op jit(solution)/shard_map/all_gather | solution.py:28
  50.7 1.5 reshape.19
  52.2 0.1 copy.22
  52.3 0.7 all_to_all.6
  53.1 0.0 copy-start.1
  53.1 1.6 copy.15
  54.6 15.0 %all-to-all-start = ((f32[32,128,64]{1,2,0:T(8,128)}), f32[32,128,64]{1,2,0:T(8,128)S(1)}, u32[]{:S(2)}, u32[]{:S(2)}) async-start(f32[32,128,64]{1,2,0:T(8,128)} %copy.15), calls=%async_computation | async-start | bytes 2097152 | tf_op jit(solution)/shard_map/all_to_all | solution.py:30
  69.7 0.0 reduce-scatter.4.cloned.1.call-start
  69.7 0.0 copy-done.1
  69.8 27.7 %all-to-all-done = f32[32,128,64]{1,2,0:T(8,128)S(1)} async-done(((f32[32,128,64]{1,2,0:T(8,128)}), f32[32,128,64]{1,2,0:T(8,128)S(1)}, u32[]{:S(2)}, u32[]{:S(2)}) %all-to-all-start) | async-done | bytes 1048608 | tf_op jit(solution)/shard_map/all_to_all | solution.py:30
  97.4 0.6 copy.16
  98.0 0.2 copy.17
  98.2 0.1 fusion
  98.3 6.1 %convolution_bitcast_fusion = f32[1024,64]{0,1:T(8,128)S(1)} fusion(bf16[4096,64]{1,0:T(8,128)(2,1)S(1)} %fusion, bf16[1024,4096]{1,0:T(8,128)(2,1)} %param.4), kind=kOutput, calls=%fused_computation.2 | convolution fusion | flops 536870912 | bytes 9175040 | tf_op jit(solution)/shard_map/dot_general | solution.py:34
  104.4 1.0 copy.19
  105.4 0.0 reduce-scatter.4.cloned.1.call-update
  105.5 0.0 all-reduce.2.cloned.1.call-start
  105.5 104.0 %reduce-scatter.4.cloned.1.call-done = f32[32,64]{1,0:T(8,128)} async-done(((f32[1024,64]{1,0:T(8,128)}), f32[32,64]{1,0:T(8,128)}) %reduce-scatter.4.cloned.1.call-update) | async-done | bytes 8208
  209.5 0.8 copy.20
  210.3 0.0 copy-done
  210.3 0.8 fusion.1
  211.0 0.0 all-reduce.2.cloned.1.call-update
  211.1 0.7 copy.18
  211.7 246.2 %all-reduce.2.cloned.1.call-done = f32[64,256]{1,0:T(8,128)} async-done(((f32[64,256]{1,0:T(8,128)}), f32[64,256]{1,0:T(8,128)}) %all-reduce.2.cloned.1.call-update) | async-done | bytes 65552 | tf_op jit(solution)/shard_map/psum | solution.py:44
  458.0 1.5 broadcast_multiply_fusion
  (1 shorter events, 0.0 us)
Async XLA Ops:
  7.2 203.1 %copy-start = (bf16[32,256]{1,0:T(8,128)(2,1)S(1)}, bf16[32,256]{1,0:T(8,128)(2,1)}, u32[]{:S(2)}) copy-start(bf16[32,256]{1,0:T(8,128)(2,1)} %param.7) | copy-start | bytes 49156
  7.2 43.5 %all-gather.2.cloned.1.call-start = ((), (), s32[]{:S(2)}) async-start(), calls=%async_computation.2 | async-start | bytes 1179648 | tf_op jit(solution)/shard_map/all_gather | solution.py:28
  53.1 16.7 %copy-start.1 = (f32[64]{0:T(128)S(1)}, f32[64]{0:T(128)}, u32[]{:S(2)}) copy-start(f32[64]{0:T(128)} %param.6) | copy-start | bytes 772
  54.6 42.8 %all-to-all-start = ((f32[32,128,64]{1,2,0:T(8,128)}), f32[32,128,64]{1,2,0:T(8,128)S(1)}, u32[]{:S(2)}, u32[]{:S(2)}) async-start(f32[32,128,64]{1,2,0:T(8,128)} %copy.15), calls=%async_computation | async-start | bytes 2097152 | tf_op jit(solution)/shard_map/all_to_all | solution.py:30
  69.7 139.8 %reduce-scatter.4.cloned.1.call-start = ((), (), s32[]{:S(2)}) async-start(), calls=%async_computation.4 | async-start | bytes 540672
  105.5 352.5 %all-reduce.2.cloned.1.call-start = ((), (), s32[]{:S(2)}) async-start(), calls=%async_computation.3 | async-start | bytes 131072 | tf_op jit(solution)/shard_map/psum | solution.py:44
Sparse Core Ops, SparseCore 0:
  9.8 40.8 all-gather.1
  105.6 103.8 reduce-scatter.3
  216.5 241.4 all-reduce.1
where the time goes:
time: 466 us
  waiting for transfers between devices  421 us (90%)
  starting transfers between devices  15.2 us (3%)
  between operations  13.8 us (3%)
  local copies, waits for them, and re-layouts  7.2 us (2%)
  matrix products  6.85 us (1%)
    psum x1, waiting for transfers between devices, per_device(): lax.psum(partial_value, ('space', 'snap')) / math.sqrt(total_cells)  246 us
    unnamed x4, waiting for transfers between devices  105 us
    all_gather x1, waiting for transfers between devices, per_device(): widened = lax.all_gather(vectors_cyclic, 'space', axis=1, tiled=True)  42.8 us
    all_to_all x1, waiting for transfers between devices, per_device(): lax.all_to_all(widened, 'snap', split_axis=0, concat_axis=0, tiled=True)  27.7 us
    all_to_all x1, starting transfers between devices, per_device(): lax.all_to_all(widened, 'snap', split_axis=0, concat_axis=0, tiled=True)  15 us
  transfers between devices with their start and end apart: 4, of which 4 were waited for; matrix products, arithmetic and copies ran while one was open for 0% of the time, Pallas kernels for 0%

commit v1 on v0

v1 whole, which is shorter than its diff:
```python
import functools
import math

import jax
import jax.numpy as jnp
from jax import lax
from jax.experimental import pallas as pl
from jax.experimental.pallas import tpu as pltpu
from jax.sharding import PartitionSpec as P

MESH = pl.DeviceIdType.MESH
ROW_BLOCK = 16
COL_BLOCK = 4
LANES = 128
SUBLANES = 8
CORES = 2
CHUNKS = 4
ROW_TILE = 256


def swap_lane_groups(tiles):
    count = len(tiles)
    lane = lax.broadcasted_iota(jnp.int32, tiles[0].shape, tiles[0].ndim - 1)
    step = 1
    while step < count:
        low = (lane // (ROW_BLOCK * step)) % 2 == 0
        fresh = list(tiles)
        for a in range(count):
            if a & step:
                continue
            x, y = tiles[a], tiles[a + step]
            fresh[a] = jnp.where(low, x, pltpu.roll(y, ROW_BLOCK * step, y.ndim - 1))
            fresh[a + step] = jnp.where(low, pltpu.roll(x, LANES - ROW_BLOCK * step, x.ndim - 1), y)
        tiles = fresh
        step *= 2
    return tiles


def mode_rows(held_rows, pairs):
    first, second = [], []
    for t in range(pairs):
        even, odd = held_rows[2 * t], held_rows[2 * t + 1]
        upper = lax.broadcasted_iota(jnp.int32, even.shape, 0) < COL_BLOCK
        first.append(jnp.where(upper, even, pltpu.roll(odd, COL_BLOCK, 0)))
        second.append(jnp.where(upper, pltpu.roll(even, COL_BLOCK, 0), odd))
    return jnp.concatenate(first + second, axis=0)


def kernel(
    n_space, n_snap, total_cells,
    s_hbm, v_hbm, ev_ref, h_hbm,
    modes_ref, coef_ref,
    s_v, h_v, recv, e_all, acc, pack, sums, c_out, c_in, d_out, d_in, f_in,
    s_sem, h_sem, a_send, a_recv, g_send, g_recv, r_send, r_recv, c_send, c_recv,
):
    q, p = lax.axis_index("space"), lax.axis_index("snap")
    core = lax.rem(p, CORES)
    n_near, n_far = n_space * CORES, n_snap // CORES
    near, far = q * CORES + core, p // CORES
    cells, snaps = s_v.shape
    modes = acc.shape[1]
    width = snaps // CHUNKS
    rows_each = cells // n_snap

    def near_id(a):
        return (a // CORES, p - core + lax.rem(a, CORES))

    def far_id(b):
        return (q, b * CORES + core)

    def s_copy(c):
        cols = pl.ds(c * width, width)
        return pltpu.make_async_copy(s_hbm.at[:, cols], s_v.at[:, cols], s_sem.at[c])

    def drain(view, sem):
        pltpu.make_async_copy(view, view, sem).wait()

    barrier = pltpu.get_barrier_semaphore()

    @pl.loop(1, n_snap)
    def _(d):
        pl.semaphore_signal(barrier, inc=1, device_id=(q, lax.rem(p + d, n_snap)), device_id_type=MESH)

    @pl.loop(1, n_space)
    def _(d):
        other = lax.rem(q + d, n_space)
        pl.semaphore_signal(barrier, inc=1, device_id=(other, p), device_id_type=MESH)
        pl.semaphore_signal(barrier, inc=1, device_id=(other, p + 1 - 2 * core), device_id_type=MESH)

    h_copy = pltpu.make_async_copy(h_hbm, h_v, h_sem)
    for c in range(CHUNKS):
        s_copy(c).start()
    h_copy.start()
    pl.semaphore_wait(barrier, n_snap - 1 + 2 * (n_space - 1))

    @pl.loop(1, n_snap)
    def _(d):
        other = lax.rem(p + d, n_snap)
        pltpu.make_async_remote_copy(
            src_ref=v_hbm.at[:, pl.ds(pl.multiple_of(other * LANES, LANES), LANES)],
            dst_ref=recv.at[p],
            send_sem=a_send,
            recv_sem=a_recv,
            device_id=(q, other),
            device_id_type=MESH,
        ).start()

    own = pltpu.make_async_copy(v_hbm.at[:, pl.ds(pl.multiple_of(p * LANES, LANES), LANES)], recv.at[p], c_send.at[3])
    own.start()
    row = lax.broadcasted_iota(jnp.int32, (SUBLANES, LANES), 0)
    values = jnp.zeros((SUBLANES, LANES), jnp.float32)
    for r in range(SUBLANES):
        value = ev_ref[((r // COL_BLOCK) * n_space + q) * COL_BLOCK + r % COL_BLOCK]
        values = jnp.where(row == r, value, values)
    scale = lax.rsqrt(values)
    own.wait()
    drain(recv.at[pl.ds(0, n_snap - 1)], a_recv)

    groups = LANES // ROW_BLOCK
    for g in range(n_snap // groups):
        tiles = swap_lane_groups([recv[g * groups + a] for a in range(groups)])
        for k in range(groups):
            at = k * n_snap * ROW_BLOCK + g * LANES
            e_all[q, :, at : at + LANES] = tiles[k] * scale

    for c in range(CHUNKS):
        cols = pl.ds(c * width, width)

        @pl.loop(1, n_space)
        def _(d):
            pltpu.make_async_remote_copy(
                src_ref=e_all.at[q, :, cols],
                dst_ref=e_all.at[q, :, cols],
                send_sem=g_send,
                recv_sem=g_recv.at[c],
                device_id=(lax.rem(q + d, n_space), p),
                device_id_type=MESH,
            ).start()

    tiles_m = cells // ROW_TILE
    targets = ROW_TILE // rows_each
    mine = p // targets
    for c in range(CHUNKS):
        cols = pl.ds(c * width, width)
        drain(e_all.at[pl.ds(0, n_space - 1), :, cols], g_recv.at[c])
        weights = mode_rows([e_all[s, :, cols] for s in range(n_space)], n_space // 2).astype(jnp.bfloat16)
        s_copy(c).wait()

        @pl.loop(0, tiles_m)
        def _(step):
            m = lax.rem(mine + 1 + step, tiles_m)
            rows = pl.ds(pl.multiple_of(m * ROW_TILE, ROW_TILE), ROW_TILE)
            value = lax.dot_general(
                s_v[rows, cols], weights, (((1,), (1,)), ((), ())), preferred_element_type=jnp.float32
            )
            if c > 0:
                value = value + acc[rows, :]
            if c < CHUNKS - 1:
                acc[rows, :] = value
            else:
                halves = value.reshape(targets, 2, rows_each // 2, modes)
                pack[pl.ds(m * targets, targets)] = jnp.concatenate([halves[:, 0], halves[:, 1]], axis=-1)

                @pl.loop(0, targets)
                def _(t):
                    other = m * targets + t

                    @pl.when(other != p)
                    def _():
                        pltpu.make_async_remote_copy(
                            src_ref=pack.at[other],
                            dst_ref=sums.at[p],
                            send_sem=r_send,
                            recv_sem=r_recv,
                            device_id=(q, other),
                            device_id_type=MESH,
                        ).start()

    sums[p] = pack[p]
    drain(sums.at[pl.ds(0, n_snap - 1)], r_recv)
    total = jnp.sum(sums[...], axis=0)
    found = jnp.concatenate([total[:, :modes], total[:, modes:]], axis=0).astype(jnp.bfloat16)
    modes_ref[...] = found

    h_copy.wait()
    partial_value = lax.dot_general(
        found, h_v[...], (((0,), (0,)), ((), ())), preferred_element_type=jnp.float32
    )
    wide = h_v.shape[1] // LANES
    for a in range(n_near):
        r, s = a // wide, a % wide
        c_out[a] = partial_value[r * SUBLANES : (r + 1) * SUBLANES, s * LANES : (s + 1) * LANES]

    @pl.loop(1, n_near)
    def _(d):
        other = lax.rem(near + d, n_near)
        pltpu.make_async_remote_copy(
            src_ref=c_out.at[other],
            dst_ref=c_in.at[near],
            send_sem=c_send.at[0],
            recv_sem=c_recv.at[0],
            device_id=near_id(other),
            device_id_type=MESH,
        ).start()

    c_in[near] = c_out[near]
    drain(c_in.at[pl.ds(0, n_near - 1)], c_recv.at[0])
    d_out[...] = jnp.sum(c_in[...], axis=0)

    @pl.loop(1, n_far)
    def _(d):
        pltpu.make_async_remote_copy(
            src_ref=d_out,
            dst_ref=d_in.at[far],
            send_sem=c_send.at[1],
            recv_sem=c_recv.at[1],
            device_id=far_id(lax.rem(far + d, n_far)),
            device_id_type=MESH,
        ).start()

    d_in[far] = d_out[...]
    drain(d_in.at[pl.ds(0, n_far - 1)], c_recv.at[1])
    f_in[near] = jnp.sum(d_in[...], axis=0) * (1.0 / math.sqrt(total_cells))

    @pl.loop(1, n_near)
    def _(d):
        pltpu.make_async_remote_copy(
            src_ref=f_in.at[near],
            dst_ref=f_in.at[near],
            send_sem=c_send.at[2],
            recv_sem=c_recv.at[2],
            device_id=near_id(lax.rem(near + d, n_near)),
            device_id_type=MESH,
        ).start()

    drain(recv.at[pl.ds(0, n_snap - 1)], a_send)
    for c in range(CHUNKS):
        drain(e_all.at[pl.ds(0, n_space - 1), :, pl.ds(c * width, width)], g_send)
    drain(pack.at[pl.ds(0, n_snap - 1)], r_send)
    drain(c_out.at[pl.ds(0, n_near - 1)], c_send.at[0])
    drain(d_in.at[pl.ds(0, n_far - 1)], c_send.at[1])
    drain(f_in.at[pl.ds(0, n_near - 1)], c_recv.at[2])
    for a in range(n_near):
        r, s = a // wide, a % wide
        coef_ref[r * SUBLANES : (r + 1) * SUBLANES, s * LANES : (s + 1) * LANES] = f_in[a]
    drain(f_in.at[pl.ds(0, n_near - 1)], c_send.at[2])


def solution(mesh):
    n_space, n_snap = mesh.shape["space"], mesh.shape["snap"]

    def per_device(snapshots, vectors_cyclic, eigen_values, held_out):
        cells, snaps = snapshots.shape
        modes, held = eigen_values.shape[0], held_out.shape[1]
        rows_each = cells // n_snap
        n_near, n_far = n_space * CORES, n_snap // CORES
        tile = (SUBLANES, LANES)
        vmem, dma = pltpu.VMEM, pltpu.SemaphoreType.DMA
        f32 = jnp.float32
        return pl.pallas_call(
            functools.partial(kernel, n_space, n_snap, cells * n_space),
            out_shape=(
                jax.ShapeDtypeStruct((rows_each, modes), jnp.bfloat16),
                jax.ShapeDtypeStruct((modes, held), f32),
            ),
            in_specs=[
                pl.BlockSpec(memory_space=pl.ANY),
                pl.BlockSpec(memory_space=pl.ANY),
                pl.BlockSpec(memory_space=pltpu.SMEM),
                pl.BlockSpec(memory_space=pl.ANY),
            ],
            out_specs=[pl.BlockSpec(memory_space=pltpu.VMEM)] * 2,
            scratch_shapes=[
                vmem((cells, snaps), jnp.bfloat16),
                vmem(held_out.shape, jnp.bfloat16),
                vmem((n_snap, *tile), f32),
                vmem((n_space, SUBLANES, snaps), f32),
                vmem((cells, modes), f32),
                vmem((n_snap, rows_each // 2, 2 * modes), f32),
                vmem((n_snap, rows_each // 2, 2 * modes), f32),
                vmem((n_near, *tile), f32),
                vmem((n_near, *tile), f32),
                vmem(tile, f32),
                vmem((n_far, *tile), f32),
                vmem((n_near, *tile), f32),
                dma((CHUNKS,)),
                dma,
                dma,
                dma,
                dma,
                dma((CHUNKS,)),
                dma,
                dma,
                dma((4,)),
                dma((3,)),
            ],
            compiler_params=pltpu.CompilerParams(
                collective_id=0, has_side_effects=True, vmem_limit_bytes=60 * 1024 * 1024
            ),
        )(snapshots, vectors_cyclic.T, eigen_values, held_out)

    return jax.shard_map(
        per_device,
        mesh=mesh,
        in_specs=(P("space", "snap"), P("snap", "space"), P(), P(("space", "snap"), None)),
        out_specs=(P(("space", "snap"), None), P()),
        check_vma=False,
    )
```

time: 466 us -> 61.7 us (0.13)
  waiting for transfers between devices: 421 us -> 0 us
  Pallas kernels: 0 us -> 58 us
  starting transfers between devices: 15.2 us -> 0 us
  between operations: 13.8 us -> 0.64 us
  matrix products: 6.85 us -> 0 us
    psum x1 -> x0, waiting for transfers between devices: 246 us -> none  [per_device(): lax.psum(partial_value, ('space', 'snap')) / math.sqrt(total_cells)]
    unnamed x4 -> x0, waiting for transfers between devices: 105 us -> none
    pallas_call x0 -> x1, Pallas kernels: none -> 58 us  [per_device(): pl.pallas_call(functools.partial(kernel, n_space, n_snap, cells * n_space...]
    all_gather x1 -> x0, waiting for transfers between devices: 42.8 us -> none  [per_device(): widened = lax.all_gather(vectors_cyclic, 'space', axis=1, tiled=True)]
    all_to_all x1 -> x0, waiting for transfers between devices: 27.7 us -> none  [per_device(): lax.all_to_all(widened, 'snap', split_axis=0, concat_axis=0, tiled=True)]
    all_to_all x1 -> x0, starting transfers between devices: 15 us -> none  [per_device(): lax.all_to_all(widened, 'snap', split_axis=0, concat_axis=0, tiled=True)]
    dot_general x2 -> x0, matrix products: 6.85 us -> none  [the longest x1 6.1 us: per_device(): jnp.dot(snapshots, scaled, preferred_element_type=jnp.float32)]
  transfers between devices with their start and end apart: 4 -> 0, of which waited for: 4 -> 0; matrix products, arithmetic and copies ran while one was open for 0% -> 0% of each run, Pallas kernels for 0% -> 0%
where the time goes in v1:
time: 61.7 us; the launch traced here: 61.5 us
  Pallas kernels  58 us (94%)
  local copies, waits for them, and re-layouts  2.77 us (4%)
  between operations  0.64 us (1%)
    pallas_call x1, Pallas kernels, per_device(): pl.pallas_call(functools.partial(kernel, n_space, n_snap, cells * n_space...  58 us
    unnamed x2, local copies, waits for them, and re-layouts  2.77 us

profile of v1, /device:TPU:1, one launch (start us, length us, event | category | flops | bytes accessed | tf_op | source)
XLA Modules:
  0.0 61.5 jit_solution(7882513101269957473)
XLA Ops:
  0.6 58.0 %shard_map.59 = (bf16[32,64]{1,0:T(8,128)(2,1)}, f32[64,256]{1,0:T(8,128)}) custom-call(bf16[1024,4096]{1,0:T(8,128)(2,1)} %s_hbm.1, f32[8,4096]{1,0:T(8,128)} %bitcast.1, f32[64]{0:T(128)} %ev_ref.1, bf16[32,256]{1,0:T(8,128)(2,1)} %h_hbm.1), custom_call_target="tpu_custom_call" | custom-call | tf_op jit(solution)/shard_map/pallas_call | solution.py:260
  58.7 1.3 %copy.8 = bf16[32,64]{1,0:T(8,128)(2,1)} copy(bf16[32,64]{1,0:T(8,128)(2,1)} %get-tuple-element.4) | data formatting | bytes 8192
  60.0 1.5 %copy.9 = f32[64,256]{1,0:T(8,128)} copy(f32[64,256]{1,0:T(8,128)} %get-tuple-element.5) | data formatting | bytes 131072

commit v2 on v1

v2 whole, which is shorter than its diff:
```python
import functools
import math

import jax
import jax.numpy as jnp
from jax import lax
from jax.experimental import pallas as pl
from jax.experimental.pallas import tpu as pltpu
from jax.sharding import PartitionSpec as P

MESH = pl.DeviceIdType.MESH
ROW_BLOCK = 16
COL_BLOCK = 4
LANES = 128
SUBLANES = 8
CORES = 2
ROW_TILE = 256
VMEM_LIMIT = 57 * 1024 * 1024
ROUTES = ("x", "y", "x", "y")


def swap_lane_groups(tiles):
    count = len(tiles)
    lane = lax.broadcasted_iota(jnp.int32, tiles[0].shape, tiles[0].ndim - 1)
    step = 1
    while step < count:
        low = (lane // (ROW_BLOCK * step)) % 2 == 0
        fresh = list(tiles)
        for a in range(count):
            if a & step:
                continue
            x, y = tiles[a], tiles[a + step]
            fresh[a] = jnp.where(low, x, pltpu.roll(y, ROW_BLOCK * step, y.ndim - 1))
            fresh[a + step] = jnp.where(low, pltpu.roll(x, LANES - ROW_BLOCK * step, x.ndim - 1), y)
        tiles = fresh
        step *= 2
    return tiles


def mode_rows(held_rows, pairs):
    first, second = [], []
    for t in range(pairs):
        even, odd = held_rows[2 * t], held_rows[2 * t + 1]
        upper = lax.broadcasted_iota(jnp.int32, even.shape, 0) < COL_BLOCK
        first.append(jnp.where(upper, even, pltpu.roll(odd, COL_BLOCK, 0)))
        second.append(jnp.where(upper, pltpu.roll(even, COL_BLOCK, 0), odd))
    return jnp.concatenate(first + second, axis=0)


def kernel(
    n_space, n_snap, total_cells,
    s_hbm, v_hbm, ev_ref, h_hbm,
    modes_ref, coef_ref,
    s_v, h_v, h_all, recv, e_all, acc, pack, partner, paired, sums, c_out, c_in, d_out, d_in, f_in,
    s_sem, h_sem, a_send, a_recv, own_sem, hy_send, hy_recv, hz_send, hz_recv, g_send, g_first, g_rest,
    k_send, k_recv, r_send, r_recv, c_send, c_recv,
):
    q, p = lax.axis_index("space"), lax.axis_index("snap")
    core = lax.rem(p, CORES)
    n_near, n_far = n_space * CORES, n_snap // CORES
    near, far = q * CORES + core, p // CORES
    n_x, n_z = n_space // 2, n_far // 2
    x, y = q // 2, lax.rem(q, 2)
    z, row_y = lax.rem(far, n_z), far // n_z
    across = 2 * x + 1 - y
    facing = (1 - row_y) * n_z + z
    cells, snaps = s_v.shape
    modes = acc.shape[1]
    groups = LANES // ROW_BLOCK
    chunks = n_snap // groups
    half = max(chunks // 2, 1)
    rows_each = cells // n_snap
    tiles_m = cells // ROW_TILE
    owners = n_far // tiles_m

    def remote(src, dst, send, arrived, space, snap):
        return pltpu.make_async_remote_copy(
            src_ref=src, dst_ref=dst, send_sem=send, recv_sem=arrived, device_id=(space, snap), device_id_type=MESH
        )

    def drain(view, sem):
        pltpu.make_async_copy(view, view, sem).wait()

    def near_id(a):
        return a // CORES, p - core + lax.rem(a, CORES)

    def group_of(o):
        if chunks == 1:
            return 0
        own_y, own_z = p // groups // half, lax.rem(p // groups, half)
        return lax.rem(own_y + o // half, 2) * half + lax.rem(own_z + o % half, half)

    barrier = pltpu.get_barrier_semaphore()

    @pl.loop(1, n_snap)
    def _(d):
        pl.semaphore_signal(barrier, inc=1, device_id=(q, lax.rem(p + d, n_snap)), device_id_type=MESH)

    @pl.loop(1, n_space)
    def _(d):
        other = lax.rem(q + d, n_space)
        pl.semaphore_signal(barrier, inc=1, device_id=(other, p), device_id_type=MESH)
        pl.semaphore_signal(barrier, inc=1, device_id=(other, p + 1 - 2 * core), device_id_type=MESH)

    own = pltpu.make_async_copy(v_hbm.at[:, pl.ds(pl.multiple_of(p * LANES, LANES), LANES)], recv.at[p], own_sem)
    own.start()
    h_copy = pltpu.make_async_copy(h_hbm, h_v, h_sem)
    h_copy.start()

    def s_copy(m):
        rows = pl.ds(m * ROW_TILE, ROW_TILE)
        return pltpu.make_async_copy(s_hbm.at[rows], s_v.at[rows], s_sem.at[m])

    for m in range(tiles_m):
        s_copy(m).start()
    row = lax.broadcasted_iota(jnp.int32, (SUBLANES, LANES), 0)
    values = jnp.zeros((SUBLANES, LANES), jnp.float32)
    for r in range(SUBLANES):
        value = ev_ref[((r // COL_BLOCK) * n_space + q) * COL_BLOCK + r % COL_BLOCK]
        values = jnp.where(row == r, value, values)
    scale = lax.rsqrt(values)
    h_copy.wait()
    h_all[far] = h_v[...].astype(jnp.float32)
    own.wait()
    pl.semaphore_wait(barrier, n_snap - 1 + 2 * (n_space - 1))

    @pl.loop(1, n_snap)
    def _(d):
        other = lax.rem(p + d, n_snap)
        cols = pl.ds(pl.multiple_of(other * LANES, LANES), LANES)
        remote(v_hbm.at[:, cols], recv.at[p], a_send, a_recv.at[p // groups], q, other).start()

    remote(h_all.at[far], h_all.at[far], hy_send, hy_recv, q, facing * CORES + core).start()

    def order_chunk(o):
        group = group_of(o)
        drain(recv.at[pl.ds(0, groups - 1 if o == 0 else groups)], a_recv.at[group])
        tiles = swap_lane_groups([recv[group * groups + a] for a in range(groups)])
        for k in range(groups):
            e_all[q, o, :, k * LANES : (k + 1) * LANES] = tiles[k] * scale

    def send_rows(source, o, sem, space):
        remote(e_all.at[source, o], e_all.at[source, o], g_send, sem, space, p).start()

    def along_x(source, o, sem):
        @pl.loop(1, n_x)
        def _(d):
            send_rows(source, o, sem, 2 * lax.rem(x + d, n_x) + y)

    def start_chunk(o):
        route = ROUTES[o]
        if route == "d":

            @pl.loop(1, n_space)
            def _(d):
                send_rows(q, o, g_rest.at[o], lax.rem(q + d, n_space))

        elif route == "y":
            send_rows(q, o, g_first.at[o], across)
            along_x(q, o, g_rest.at[o])
        else:
            along_x(q, o, g_first.at[o])
            send_rows(q, o, g_rest.at[o], across)

    def relay_chunk(o):
        route = ROUTES[o]
        if route == "y":
            drain(e_all.at[0, o], g_first.at[o])
            along_x(across, o, g_rest.at[o])
        elif route == "x" and n_x > 1:
            drain(e_all.at[pl.ds(0, n_x - 1), o], g_first.at[o])

            @pl.loop(1, n_x)
            def _(d):
                send_rows(2 * lax.rem(x + d, n_x) + y, o, g_rest.at[o], across)

    def multiply_chunk(o):
        rest = {"d": n_space - 1, "y": 2 * (n_x - 1), "x": n_x}[ROUTES[o]]
        if rest:
            drain(e_all.at[pl.ds(0, rest), o], g_rest.at[o])
        weights = mode_rows([e_all[s, o] for s in range(n_space)], n_space // 2).astype(jnp.bfloat16)
        group = group_of(o)

        @pl.loop(0, tiles_m)
        def _(m):
            rows = pl.ds(pl.multiple_of(m * ROW_TILE, ROW_TILE), ROW_TILE)
            parts = []
            for k in range(groups):
                at = pl.multiple_of(k * n_snap * ROW_BLOCK + group * LANES, LANES)
                parts.append(s_v[rows, pl.ds(at, LANES)])
            value = lax.dot_general(
                jnp.concatenate(parts, axis=1), weights, (((1,), (1,)), ((), ())), preferred_element_type=jnp.float32
            )
            if o > 0:
                value = value + acc[rows, :]
            if o < chunks - 1:
                acc[rows, :] = value
            else:
                split = value.reshape(owners, CORES, 2, rows_each // 2, modes)
                mine = pl.ds(m * owners, owners)
                for c in range(CORES):
                    pack[c, mine] = jnp.concatenate([split[:, c, 0], split[:, c, 1]], axis=-1)
                remote(
                    pack.at[1 - core, mine], partner.at[mine], k_send, k_recv.at[m], q, p + 1 - 2 * core
                ).start()

    def send_held():
        drain(h_all.at[0], hy_recv)

        @pl.loop(1, n_z)
        def _(d):
            other = lax.rem(z + d, n_z) + row_y * n_z
            for slot in (far, facing):
                remote(h_all.at[slot], h_all.at[slot], hz_send, hz_recv, q, other * CORES + core).start()

    for o in range(chunks):
        order_chunk(o)
        start_chunk(o)
        if o == 0:
            send_held()
        if o >= 2:
            relay_chunk(o - 2)
    for o in range(max(chunks - 2, 0), chunks):
        relay_chunk(o)
        if o == chunks - 2:
            for m in range(tiles_m):
                s_copy(m).wait()
            multiply_chunk(0)
    if chunks == 1:
        for m in range(tiles_m):
            s_copy(m).wait()
        multiply_chunk(0)
    for o in range(1, chunks):
        multiply_chunk(o)

    @pl.loop(0, tiles_m)
    def _(m):
        mine = pl.ds(m * owners, owners)
        drain(partner.at[mine], k_recv.at[m])
        paired[mine] = pack[core, mine] + partner[mine]

        @pl.loop(0, owners)
        def _(t):
            other = m * owners + t

            @pl.when(other != far)
            def _():
                remote(paired.at[other], sums.at[far], r_send, r_recv, q, other * CORES + core).start()

    drain(h_all.at[pl.ds(0, 2 * (n_z - 1))], hz_recv)
    partial_value = None
    for s in range(2):
        found = paired[:, :, s * modes : (s + 1) * modes].reshape(n_far * rows_each // 2, modes)
        held = h_all[:, s * rows_each // 2 : (s + 1) * rows_each // 2, :].reshape(n_far * rows_each // 2, h_v.shape[1])
        held = held.astype(jnp.bfloat16)
        upper = found.astype(jnp.bfloat16)
        lower = (found - upper.astype(jnp.float32)).astype(jnp.bfloat16)
        for piece in (upper, lower):
            term = lax.dot_general(piece, held, (((0,), (0,)), ((), ())), preferred_element_type=jnp.float32)
            partial_value = term if partial_value is None else partial_value + term
    wide = h_v.shape[1] // LANES
    for a in range(n_near):
        r, s = a // wide, a % wide
        c_out[a] = partial_value[r * SUBLANES : (r + 1) * SUBLANES, s * LANES : (s + 1) * LANES]

    @pl.loop(1, n_near)
    def _(d):
        other = lax.rem(near + d, n_near)
        remote(c_out.at[other], c_in.at[near], c_send.at[0], c_recv.at[0], *near_id(other)).start()

    c_in[near] = c_out[near]
    drain(c_in.at[pl.ds(0, n_near - 1)], c_recv.at[0])
    d_out[...] = jnp.sum(c_in[...], axis=0)

    @pl.loop(1, n_far)
    def _(d):
        other = lax.rem(far + d, n_far)
        remote(d_out, d_in.at[far], c_send.at[1], c_recv.at[1], q, other * CORES + core).start()

    d_in[far] = d_out[...]
    sums[far] = paired[far]
    drain(sums.at[pl.ds(0, n_far - 1)], r_recv)
    modes_ref[...] = jnp.sum(sums[...], axis=0)
    drain(d_in.at[pl.ds(0, n_far - 1)], c_recv.at[1])
    f_in[near] = jnp.sum(d_in[...], axis=0) * (1.0 / math.sqrt(total_cells))

    @pl.loop(1, n_near)
    def _(d):
        other = lax.rem(near + d, n_near)
        remote(f_in.at[near], f_in.at[near], c_send.at[2], c_recv.at[2], *near_id(other)).start()

    drain(recv.at[pl.ds(0, n_snap - 1)], a_send)
    drain(h_all.at[0], hy_send)
    drain(h_all.at[pl.ds(0, 2 * (n_z - 1))], hz_send)
    for o in range(chunks):
        drain(e_all.at[pl.ds(0, n_space - 1), o], g_send)
    drain(partner, k_send)
    drain(sums.at[pl.ds(0, n_far - 1)], r_send)
    drain(c_out.at[pl.ds(0, n_near - 1)], c_send.at[0])
    drain(d_in.at[pl.ds(0, n_far - 1)], c_send.at[1])
    drain(f_in.at[pl.ds(0, n_near - 1)], c_recv.at[2])
    coef_ref[...] = f_in[...]
    drain(f_in.at[pl.ds(0, n_near - 1)], c_send.at[2])


def place(total_ref, tiles_ref, modes_ref, coef_ref):
    modes = modes_ref.shape[1]
    half = modes_ref.shape[0] // 2
    modes_ref[:half, :] = total_ref[:, :modes].astype(jnp.bfloat16)
    modes_ref[half:, :] = total_ref[:, modes:].astype(jnp.bfloat16)
    wide = coef_ref.shape[1] // LANES
    for a in range(tiles_ref.shape[0]):
        r, s = a // wide, a % wide
        coef_ref[r * SUBLANES : (r + 1) * SUBLANES, s * LANES : (s + 1) * LANES] = tiles_ref[a]


def solution(mesh):
    n_space, n_snap = mesh.shape["space"], mesh.shape["snap"]

    def per_device(snapshots, vectors_cyclic, eigen_values, held_out):
        cells, snaps = snapshots.shape
        modes, held = eigen_values.shape[0], held_out.shape[1]
        rows_each = cells // n_snap
        n_near, n_far = n_space * CORES, n_snap // CORES
        chunks = n_snap * ROW_BLOCK // LANES
        tile = (SUBLANES, LANES)
        packed = (rows_each // 2, 2 * modes)
        vmem, dma = pltpu.VMEM, pltpu.SemaphoreType.DMA
        f32 = jnp.float32
        total, tiles = pl.pallas_call(
            functools.partial(kernel, n_space, n_snap, cells * n_space),
            out_shape=(vmem(packed, f32), vmem((n_near, *tile), f32)),
            in_specs=[
                pl.BlockSpec(memory_space=pl.ANY),
                pl.BlockSpec(memory_space=pl.ANY),
                pl.BlockSpec(memory_space=pltpu.SMEM),
                pl.BlockSpec(memory_space=pl.ANY),
            ],
            out_specs=[pl.BlockSpec(memory_space=pltpu.VMEM)] * 2,
            scratch_shapes=[
                vmem((cells, snaps), jnp.bfloat16),
                vmem(held_out.shape, jnp.bfloat16),
                vmem((n_far, *held_out.shape), f32),
                vmem((n_snap, *tile), f32),
                vmem((n_space, chunks, SUBLANES, snaps // chunks), f32),
                vmem((cells, modes), f32),
                vmem((CORES, n_far, *packed), f32),
                vmem((n_far, *packed), f32),
                vmem((n_far, *packed), f32),
                vmem((n_far, *packed), f32),
                vmem((n_near, *tile), f32),
                vmem((n_near, *tile), f32),
                vmem(tile, f32),
                vmem((n_far, *tile), f32),
                vmem((n_near, *tile), f32),
                dma((cells // ROW_TILE,)),
                dma,
                dma,
                dma((chunks,)),
                dma,
                dma,
                dma,
                dma,
                dma,
                dma,
                dma((chunks,)),
                dma((chunks,)),
                dma,
                dma((cells // ROW_TILE,)),
                dma,
                dma,
                dma((3,)),
                dma((3,)),
            ],
            compiler_params=pltpu.CompilerParams(
                collective_id=0, has_side_effects=True, vmem_limit_bytes=VMEM_LIMIT
            ),
        )(snapshots, vectors_cyclic.T, eigen_values, held_out)
        return pl.pallas_call(
            place,
            out_shape=(
                jax.ShapeDtypeStruct((rows_each, modes), jnp.bfloat16),
                jax.ShapeDtypeStruct((modes, held), f32),
            ),
            in_specs=[pl.BlockSpec(memory_space=pltpu.VMEM)] * 2,
            out_specs=[pl.BlockSpec(memory_space=pltpu.VMEM)] * 2,
            compiler_params=pltpu.CompilerParams(vmem_limit_bytes=2 * 1024 * 1024),
        )(total, tiles)

    return jax.shard_map(
        per_device,
        mesh=mesh,
        in_specs=(P("space", "snap"), P("snap", "space"), P(), P(("space", "snap"), None)),
        out_specs=(P(("space", "snap"), None), P()),
        check_vma=False,
    )
```

time: 61.7 us -> 49.1 us (0.80)
  Pallas kernels: 58 us -> 48.4 us
  local copies, waits for them, and re-layouts: 2.77 us -> 0 us
    pallas_call x1, Pallas kernels: 58 us -> 47.7 us  [per_device(): pl.pallas_call(functools.partial(kernel, n_space, n_snap, cells * n_space...]
    unnamed x2 -> x0, local copies, waits for them, and re-layouts: 2.77 us -> none
    pallas_call x0 -> x1, Pallas kernels: none -> 0.67 us  [per_device(): pl.pallas_call(place, out_shape=(jax.ShapeDtypeStruct((rows_each, modes),...]
where the time goes in v2:
time: 49.1 us; the launch traced here: 49 us
  Pallas kernels  48.4 us (99%)
  between operations  0.64 us (1%)
    pallas_call x1, Pallas kernels, per_device(): pl.pallas_call(functools.partial(kernel, n_space, n_snap, cells * n_space...  47.7 us

profile of v2, /device:TPU:1, one launch (start us, length us, event | category | flops | bytes accessed | tf_op | source)
XLA Modules:
  0.0 49.0 jit_solution(7918846355022613790)
XLA Ops:
  0.6 47.7 %shard_map.59 = (f32[16,128]{1,0:T(8,128)S(1)}, f32[16,8,128]{2,1,0:T(8,128)S(1)}) custom-call(bf16[1024,4096]{1,0:T(8,128)(2,1)} %s_hbm.1, f32[8,4096]{1,0:T(8,128)} %bitcast.1, f32[64]{0:T(128)} %ev_ref.1, bf16[32,256]{1,0:T(8,128)(2,1)} %h_hbm.1), custom_call_target="tpu_custom_call" | custom-call | tf_op jit(solution)/shard_map/pallas_call | solution.py:330
  48.3 0.7 %shard_map.60 = (bf16[32,64]{1,0:T(8,128)(2,1)}, f32[64,256]{1,0:T(8,128)}) custom-call(f32[16,128]{1,0:T(8,128)S(1)} %get-tuple-element.4.total_ref, f32[16,8,128]{2,1,0:T(8,128)S(1)} %get-tuple-element.5.tiles_ref), custom_call_target="tpu_custom_call" | custom-call | tf_op jit(solution)/shard_map/pallas_call | solution.py:379

commit v3 on v2

--- a/solution.py
+++ b/solution.py
@@ -16,7 +16,10 @@
 CORES = 2
 ROW_TILE = 256
 VMEM_LIMIT = 57 * 1024 * 1024
-ROUTES = ("x", "y", "x", "y")
+OWN_ROUTES = ("x", "x")
+OVER_ROUTES = ("y", "y")
+HB_OWN = 2
+HB_FACING = 3
 
 
 def swap_lane_groups(tiles):
@@ -49,26 +52,27 @@
 
 def kernel(
     n_space, n_snap, total_cells,
-    s_hbm, v_hbm, ev_ref, h_hbm,
+    s_hbm, v_hbm, ev_hbm, h_hbm,
     modes_ref, coef_ref,
-    s_v, h_v, h_all, recv, e_all, acc, pack, partner, paired, sums, c_out, c_in, d_out, d_in, f_in,
-    s_sem, h_sem, a_send, a_recv, own_sem, hy_send, hy_recv, hz_send, hz_recv, g_send, g_first, g_rest,
+    s_v, h_v, ev_ref, h_all, recv, staged, e_all, acc, pack, partner, paired, sums, c_out, c_in, d_out, d_in, f_in,
+    s_sem, h_sem, ev_sem, a_send, a_recv, own_sem, hy_send, hy_recv, hz_send, hz_first, hz_rest, g_send, g_first, g_rest,
     k_send, k_recv, r_send, r_recv, c_send, c_recv,
 ):
     q, p = lax.axis_index("space"), lax.axis_index("snap")
     core = lax.rem(p, CORES)
-    n_near, n_far = n_space * CORES, n_snap // CORES
-    near, far = q * CORES + core, p // CORES
+    n_near, n_far = n_space * 2, n_snap // 2
+    far = p // CORES
     n_x, n_z = n_space // 2, n_far // 2
     x, y = q // 2, lax.rem(q, 2)
     z, row_y = lax.rem(far, n_z), far // n_z
     across = 2 * x + 1 - y
     facing = (1 - row_y) * n_z + z
+    near, line = row_y * n_space + q, z * CORES + core
     cells, snaps = s_v.shape
     modes = acc.shape[1]
     groups = LANES // ROW_BLOCK
     chunks = n_snap // groups
-    half = max(chunks // 2, 1)
+    parts = chunks // 2
     rows_each = cells // n_snap
     tiles_m = cells // ROW_TILE
     owners = n_far // tiles_m
@@ -82,13 +86,14 @@
         pltpu.make_async_copy(view, view, sem).wait()
 
     def near_id(a):
-        return a // CORES, p - core + lax.rem(a, CORES)
+        return lax.rem(a, n_space), (a // n_space) * n_far + line
+
+    def part_of(i):
+        return lax.rem(line // groups + i, parts)
 
     def group_of(o):
-        if chunks == 1:
-            return 0
-        own_y, own_z = p // groups // half, lax.rem(p // groups, half)
-        return lax.rem(own_y + o // half, 2) * half + lax.rem(own_z + o % half, half)
+        t, i = o // parts, o % parts
+        return lax.rem(row_y + t, 2) * parts + part_of(i)
 
     barrier = pltpu.get_barrier_semaphore()
 
@@ -100,10 +105,16 @@
     def _(d):
         other = lax.rem(q + d, n_space)
         pl.semaphore_signal(barrier, inc=1, device_id=(other, p), device_id_type=MESH)
-        pl.semaphore_signal(barrier, inc=1, device_id=(other, p + 1 - 2 * core), device_id_type=MESH)
-
-    own = pltpu.make_async_copy(v_hbm.at[:, pl.ds(pl.multiple_of(p * LANES, LANES), LANES)], recv.at[p], own_sem)
-    own.start()
+        pl.semaphore_signal(barrier, inc=1, device_id=(other, facing * CORES + core), device_id_type=MESH)
+
+    ev_copy = pltpu.make_async_copy(ev_hbm, ev_ref, ev_sem)
+    ev_copy.start()
+    own = []
+    for t in range(2):
+        target = lax.rem(row_y + t, 2) * n_far + line
+        cols = pl.ds(pl.multiple_of(target * LANES, LANES), LANES)
+        own.append(pltpu.make_async_copy(v_hbm.at[:, cols], recv.at[t, line], own_sem.at[t]))
+        own[t].start()
     h_copy = pltpu.make_async_copy(h_hbm, h_v, h_sem)
     h_copy.start()
 
@@ -114,6 +125,7 @@
     for m in range(tiles_m):
         s_copy(m).start()
     row = lax.broadcasted_iota(jnp.int32, (SUBLANES, LANES), 0)
+    ev_copy.wait()
     values = jnp.zeros((SUBLANES, LANES), jnp.float32)
     for r in range(SUBLANES):
         value = ev_ref[((r // COL_BLOCK) * n_space + q) * COL_BLOCK + r % COL_BLOCK]
@@ -121,23 +133,37 @@
     scale = lax.rsqrt(values)
     h_copy.wait()
     h_all[far] = h_v[...].astype(jnp.float32)
-    own.wait()
+    for t in range(2):
+        own[t].wait()
     pl.semaphore_wait(barrier, n_snap - 1 + 2 * (n_space - 1))
 
-    @pl.loop(1, n_snap)
-    def _(d):
-        other = lax.rem(p + d, n_snap)
-        cols = pl.ds(pl.multiple_of(other * LANES, LANES), LANES)
-        remote(v_hbm.at[:, cols], recv.at[p], a_send, a_recv.at[p // groups], q, other).start()
+    @pl.loop(1, n_far)
+    def _(d):
+        other = lax.rem(line + d, n_far)
+        for t in range(2):
+            target = lax.rem(row_y + t, 2) * n_far + other
+            cols = pl.ds(pl.multiple_of(target * LANES, LANES), LANES)
+            remote(
+                v_hbm.at[:, cols], recv.at[t, line], a_send, a_recv.at[line // groups], q, row_y * n_far + other
+            ).start()
 
     remote(h_all.at[far], h_all.at[far], hy_send, hy_recv, q, facing * CORES + core).start()
 
-    def order_chunk(o):
-        group = group_of(o)
-        drain(recv.at[pl.ds(0, groups - 1 if o == 0 else groups)], a_recv.at[group])
-        tiles = swap_lane_groups([recv[group * groups + a] for a in range(groups)])
-        for k in range(groups):
-            e_all[q, o, :, k * LANES : (k + 1) * LANES] = tiles[k] * scale
+    def route_of(o):
+        return OWN_ROUTES[o] if o < parts else OVER_ROUTES[o - parts]
+
+    def order_part(i):
+        part = part_of(i)
+        count = groups - 1 if i == 0 else groups
+        drain(recv.at[:, pl.ds(0, count)], a_recv.at[part])
+        for t in range(2):
+            tiles = swap_lane_groups([recv[t, part * groups + a] for a in range(groups)])
+            for k in range(groups):
+                cols = slice(k * LANES, (k + 1) * LANES)
+                if t == 0:
+                    e_all[q, i, :, cols] = tiles[k] * scale
+                else:
+                    staged[i, :, cols] = tiles[k] * scale
 
     def send_rows(source, o, sem, space):
         remote(e_all.at[source, o], e_all.at[source, o], g_send, sem, space, p).start()
@@ -147,9 +173,24 @@
         def _(d):
             send_rows(source, o, sem, 2 * lax.rem(x + d, n_x) + y)
 
+    def send_over(o, sem, space):
+        remote(
+            staged.at[o - parts], e_all.at[q, o], g_send, sem, space, facing * CORES + core
+        ).start()
+
     def start_chunk(o):
-        route = ROUTES[o]
-        if route == "d":
+        route = route_of(o)
+        if o >= parts:
+            if route == "y":
+                send_over(o, g_first.at[o], q)
+                send_over(o, g_first.at[o], across)
+            else:
+
+                @pl.loop(0, n_space)
+                def _(d):
+                    send_over(o, g_rest.at[o], lax.rem(q + d, n_space))
+
+        elif route == "d":
 
             @pl.loop(1, n_space)
             def _(d):
@@ -163,8 +204,12 @@
             send_rows(q, o, g_rest.at[o], across)
 
     def relay_chunk(o):
-        route = ROUTES[o]
-        if route == "y":
+        route = route_of(o)
+        if o >= parts and route == "y":
+            drain(e_all.at[pl.ds(0, 2), o], g_first.at[o])
+            along_x(q, o, g_rest.at[o])
+            along_x(across, o, g_rest.at[o])
+        elif route == "y":
             drain(e_all.at[0, o], g_first.at[o])
             along_x(across, o, g_rest.at[o])
         elif route == "x" and n_x > 1:
@@ -175,7 +220,7 @@
                 send_rows(2 * lax.rem(x + d, n_x) + y, o, g_rest.at[o], across)
 
     def multiply_chunk(o):
-        rest = {"d": n_space - 1, "y": 2 * (n_x - 1), "x": n_x}[ROUTES[o]]
+        rest = {"d": n_space - (o < parts), "y": 2 * (n_x - 1), "x": n_x}[route_of(o)]
         if rest:
             drain(e_all.at[pl.ds(0, rest), o], g_rest.at[o])
         weights = mode_rows([e_all[s, o] for s in range(n_space)], n_space // 2).astype(jnp.bfloat16)
@@ -204,33 +249,46 @@
                     pack.at[1 - core, mine], partner.at[mine], k_send, k_recv.at[m], q, p + 1 - 2 * core
                 ).start()
 
-    def send_held():
-        drain(h_all.at[0], hy_recv)
-
-        @pl.loop(1, n_z)
-        def _(d):
-            other = lax.rem(z + d, n_z) + row_y * n_z
-            for slot in (far, facing):
-                remote(h_all.at[slot], h_all.at[slot], hz_send, hz_recv, q, other * CORES + core).start()
-
+    far_ring = n_z == 8
+    reach = (1, 2, n_z - 1, n_z - 2) if far_ring else tuple(range(1, n_z))
+
+    def send_held(kind, source, hop, sem):
+        slot = lax.rem(row_y + kind, 2) * n_z + lax.rem(z + source, n_z)
+        target = row_y * n_z + lax.rem(z + hop, n_z)
+        remote(h_all.at[slot], h_all.at[slot], hz_send, sem, q, target * CORES + core).start()
+
+    def start_held(kind):
+        for hop in reach:
+            send_held(kind, 0, hop, hz_first.at[kind])
+
+    def relay_held(kind):
+        drain(h_all.at[pl.ds(0, len(reach))], hz_first.at[kind])
+        if far_ring:
+            hops = ((n_z - 2, 1), (2, n_z - 1), (n_z - 2, 2) if kind == 0 else (2, n_z - 2))
+            for source, hop in hops:
+                send_held(kind, source, hop, hz_rest.at[kind])
+
+    def finish_held():
+        if far_ring:
+            for kind in range(2):
+                drain(h_all.at[pl.ds(0, 3)], hz_rest.at[kind])
+
+    start_held(0)
+    for i in range(parts):
+        order_part(i)
+        start_chunk(i)
+        start_chunk(parts + i)
+        if i == 0:
+            drain(h_all.at[0], hy_recv)
+            start_held(1)
+    steps = [functools.partial(relay_chunk, o) for i in range(parts) for o in (i, parts + i)]
+    steps.insert(HB_OWN if parts > 1 else 0, functools.partial(relay_held, 0))
+    steps.insert(HB_FACING if parts > 1 else 1, functools.partial(relay_held, 1))
+    for step in steps:
+        step()
+    for m in range(tiles_m):
+        s_copy(m).wait()
     for o in range(chunks):
-        order_chunk(o)
-        start_chunk(o)
-        if o == 0:
-            send_held()
-        if o >= 2:
-            relay_chunk(o - 2)
-    for o in range(max(chunks - 2, 0), chunks):
-        relay_chunk(o)
-        if o == chunks - 2:
-            for m in range(tiles_m):
-                s_copy(m).wait()
-            multiply_chunk(0)
-    if chunks == 1:
-        for m in range(tiles_m):
-            s_copy(m).wait()
-        multiply_chunk(0)
-    for o in range(1, chunks):
         multiply_chunk(o)
 
     @pl.loop(0, tiles_m)
@@ -239,15 +297,7 @@
         drain(partner.at[mine], k_recv.at[m])
         paired[mine] = pack[core, mine] + partner[mine]
 
-        @pl.loop(0, owners)
-        def _(t):
-            other = m * owners + t
-
-            @pl.when(other != far)
-            def _():
-                remote(paired.at[other], sums.at[far], r_send, r_recv, q, other * CORES + core).start()
-
-    drain(h_all.at[pl.ds(0, 2 * (n_z - 1))], hz_recv)
+    finish_held()
     partial_value = None
     for s in range(2):
         found = paired[:, :, s * modes : (s + 1) * modes].reshape(n_far * rows_each // 2, modes)
@@ -268,16 +318,21 @@
         other = lax.rem(near + d, n_near)
         remote(c_out.at[other], c_in.at[near], c_send.at[0], c_recv.at[0], *near_id(other)).start()
 
+    @pl.loop(1, n_far)
+    def _(d):
+        other = lax.rem(far + d, n_far)
+        remote(paired.at[other], sums.at[far], r_send, r_recv, q, other * CORES + core).start()
+
     c_in[near] = c_out[near]
     drain(c_in.at[pl.ds(0, n_near - 1)], c_recv.at[0])
     d_out[...] = jnp.sum(c_in[...], axis=0)
 
     @pl.loop(1, n_far)
     def _(d):
-        other = lax.rem(far + d, n_far)
-        remote(d_out, d_in.at[far], c_send.at[1], c_recv.at[1], q, other * CORES + core).start()
-
-    d_in[far] = d_out[...]
+        other = lax.rem(line + d, n_far)
+        remote(d_out, d_in.at[line], c_send.at[1], c_recv.at[1], q, row_y * n_far + other).start()
+
+    d_in[line] = d_out[...]
     sums[far] = paired[far]
     drain(sums.at[pl.ds(0, n_far - 1)], r_recv)
     modes_ref[...] = jnp.sum(sums[...], axis=0)
@@ -289,11 +344,11 @@
         other = lax.rem(near + d, n_near)
         remote(f_in.at[near], f_in.at[near], c_send.at[2], c_recv.at[2], *near_id(other)).start()
 
-    drain(recv.at[pl.ds(0, n_snap - 1)], a_send)
+    drain(recv.at[:, pl.ds(0, n_far - 1)], a_send)
     drain(h_all.at[0], hy_send)
     drain(h_all.at[pl.ds(0, 2 * (n_z - 1))], hz_send)
     for o in range(chunks):
-        drain(e_all.at[pl.ds(0, n_space - 1), o], g_send)
+        drain(e_all.at[pl.ds(0, n_space - (o < parts)), o], g_send)
     drain(partner, k_send)
     drain(sums.at[pl.ds(0, n_far - 1)], r_send)
     drain(c_out.at[pl.ds(0, n_near - 1)], c_send.at[0])
@@ -321,7 +376,7 @@
         cells, snaps = snapshots.shape
         modes, held = eigen_values.shape[0], held_out.shape[1]
         rows_each = cells // n_snap
-        n_near, n_far = n_space * CORES, n_snap // CORES
+        n_near, n_far = n_space * 2, n_snap // 2
         chunks = n_snap * ROW_BLOCK // LANES
         tile = (SUBLANES, LANES)
         packed = (rows_each // 2, 2 * modes)
@@ -333,15 +388,17 @@
             in_specs=[
                 pl.BlockSpec(memory_space=pl.ANY),
                 pl.BlockSpec(memory_space=pl.ANY),
-                pl.BlockSpec(memory_space=pltpu.SMEM),
+                pl.BlockSpec(memory_space=pl.ANY),
                 pl.BlockSpec(memory_space=pl.ANY),
             ],
             out_specs=[pl.BlockSpec(memory_space=pltpu.VMEM)] * 2,
             scratch_shapes=[
                 vmem((cells, snaps), jnp.bfloat16),
                 vmem(held_out.shape, jnp.bfloat16),
+                pltpu.SMEM((modes,), f32),
                 vmem((n_far, *held_out.shape), f32),
-                vmem((n_snap, *tile), f32),
+                vmem((2, n_far, *tile), f32),
+                vmem((chunks // 2, SUBLANES, snaps // chunks), f32),
                 vmem((n_space, chunks, SUBLANES, snaps // chunks), f32),
                 vmem((cells, modes), f32),
                 vmem((CORES, n_far, *packed), f32),
@@ -356,12 +413,14 @@
                 dma((cells // ROW_TILE,)),
                 dma,
                 dma,
-                dma((chunks,)),
-                dma,
-                dma,
-                dma,
-                dma,
-                dma,
+                dma,
+                dma((chunks // 2,)),
+                dma((2,)),
+                dma,
+                dma,
+                dma,
+                dma((2,)),
+                dma((2,)),
                 dma,
                 dma((chunks,)),
                 dma((chunks,)),

time: 49.1 us -> 47.8 us (0.974)
  Pallas kernels: 48.4 us -> 47 us
    pallas_call x1, Pallas kernels: 47.7 us -> 46.4 us  [per_device(): pl.pallas_call(functools.partial(kernel, n_space, n_snap, cells * n_space...]
where the time goes in v3:
time: 47.8 us; the launch traced here: 47.7 us
  Pallas kernels  47 us (98%)
  between operations  0.64 us (1%)
    pallas_call x1, Pallas kernels, per_device(): pl.pallas_call(functools.partial(kernel, n_space, n_snap, cells * n_space...  46.4 us

profile of v3, /device:TPU:1, one launch (start us, length us, event | category | flops | bytes accessed | tf_op | source)
XLA Modules:
  0.0 47.7 jit_solution(12346050975905110131)
XLA Ops:
  0.6 46.4 %shard_map.59 = (f32[16,128]{1,0:T(8,128)S(1)}, f32[16,8,128]{2,1,0:T(8,128)S(1)}) custom-call(bf16[1024,4096]{1,0:T(8,128)(2,1)} %s_hbm.1, f32[8,4096]{1,0:T(8,128)} %bitcast.1, f32[64]{0:T(128)} %ev_hbm.1, bf16[32,256]{1,0:T(8,128)(2,1)} %h_hbm.1), custom_call_target="tpu_custom_call" | custom-call | tf_op jit(solution)/shard_map/pallas_call | solution.py:385
  47.0 0.7 %shard_map.60 = (bf16[32,64]{1,0:T(8,128)(2,1)}, f32[64,256]{1,0:T(8,128)}) custom-call(f32[16,128]{1,0:T(8,128)S(1)} %get-tuple-element.4.total_ref, f32[16,8,128]{2,1,0:T(8,128)S(1)} %get-tuple-element.5.tiles_ref), custom_call_target="tpu_custom_call" | custom-call | tf_op jit(solution)/shard_map/pallas_call | solution.py:438

commit v4 on v3

--- a/solution.py
+++ b/solution.py
@@ -14,12 +14,12 @@
 LANES = 128
 SUBLANES = 8
 CORES = 2
-ROW_TILE = 256
+ROW_TILE = 512
 VMEM_LIMIT = 57 * 1024 * 1024
 OWN_ROUTES = ("x", "x")
 OVER_ROUTES = ("y", "y")
-HB_OWN = 2
-HB_FACING = 3
+STEPS = "r0 r2 h0 h1 r1 r3 m0 m2 m1 m3"
+FIRST_STEPS = ""
 
 
 def swap_lane_groups(tiles):
@@ -219,7 +219,7 @@
             def _(d):
                 send_rows(2 * lax.rem(x + d, n_x) + y, o, g_rest.at[o], across)
 
-    def multiply_chunk(o):
+    def multiply_chunk(o, first, last):
         rest = {"d": n_space - (o < parts), "y": 2 * (n_x - 1), "x": n_x}[route_of(o)]
         if rest:
             drain(e_all.at[pl.ds(0, rest), o], g_rest.at[o])
@@ -236,9 +236,9 @@
             value = lax.dot_general(
                 jnp.concatenate(parts, axis=1), weights, (((1,), (1,)), ((), ())), preferred_element_type=jnp.float32
             )
-            if o > 0:
+            if not first:
                 value = value + acc[rows, :]
-            if o < chunks - 1:
+            if not last:
                 acc[rows, :] = value
             else:
                 split = value.reshape(owners, CORES, 2, rows_each // 2, modes)
@@ -273,6 +273,21 @@
             for kind in range(2):
                 drain(h_all.at[pl.ds(0, 3)], hz_rest.at[kind])
 
+    def run(steps):
+        for name in steps.split():
+            at = int(name[1])
+            if name[0] == "h":
+                relay_held(at)
+            elif at < chunks and name[0] == "r":
+                relay_chunk(at)
+            elif at < chunks:
+                if not done:
+                    for m in range(tiles_m):
+                        s_copy(m).wait()
+                done.append(at)
+                multiply_chunk(at, len(done) == 1, len(done) == chunks)
+
+    done = []
     start_held(0)
     for i in range(parts):
         order_part(i)
@@ -281,15 +296,9 @@
         if i == 0:
             drain(h_all.at[0], hy_recv)
             start_held(1)
-    steps = [functools.partial(relay_chunk, o) for i in range(parts) for o in (i, parts + i)]
-    steps.insert(HB_OWN if parts > 1 else 0, functools.partial(relay_held, 0))
-    steps.insert(HB_FACING if parts > 1 else 1, functools.partial(relay_held, 1))
-    for step in steps:
-        step()
-    for m in range(tiles_m):
-        s_copy(m).wait()
-    for o in range(chunks):
-        multiply_chunk(o)
+            if parts > 1:
+                run(FIRST_STEPS)
+    run(STEPS)
 
     @pl.loop(0, tiles_m)
     def _(m):

time: 47.8 us -> 46.5 us (0.973)
  Pallas kernels: 47 us -> 45.8 us
    pallas_call x1, Pallas kernels: 46.4 us -> 45.1 us  [per_device(): pl.pallas_call(functools.partial(kernel, n_space, n_snap, cells * n_space...]
where the time goes in v4:
time: 46.5 us; the launch traced here: 46.4 us
  Pallas kernels  45.8 us (98%)
  between operations  0.64 us (1%)
    pallas_call x1, Pallas kernels, per_device(): pl.pallas_call(functools.partial(kernel, n_space, n_snap, cells * n_space...  45.1 us

profile of v4, /device:TPU:1, one launch (start us, length us, event | category | flops | bytes accessed | tf_op | source)
XLA Modules:
  0.0 46.4 jit_solution(17738718551501805369)
XLA Ops:
  0.6 45.1 %shard_map.59 = (f32[16,128]{1,0:T(8,128)S(1)}, f32[16,8,128]{2,1,0:T(8,128)S(1)}) custom-call(bf16[1024,4096]{1,0:T(8,128)(2,1)} %s_hbm.1, f32[8,4096]{1,0:T(8,128)} %bitcast.1, f32[64]{0:T(128)} %ev_hbm.1, bf16[32,256]{1,0:T(8,128)(2,1)} %h_hbm.1), custom_call_target="tpu_custom_call" | custom-call | tf_op jit(solution)/shard_map/pallas_call | solution.py:394
  45.8 0.7 %shard_map.60 = (bf16[32,64]{1,0:T(8,128)(2,1)}, f32[64,256]{1,0:T(8,128)}) custom-call(f32[16,128]{1,0:T(8,128)S(1)} %get-tuple-element.4.total_ref, f32[16,8,128]{2,1,0:T(8,128)S(1)} %get-tuple-element.5.tiles_ref), custom_call_target="tpu_custom_call" | custom-call | tf_op jit(solution)/shard_map/pallas_call | solution.py:447

commit v5 on v4

--- a/solution.py
+++ b/solution.py
@@ -18,8 +18,7 @@
 VMEM_LIMIT = 57 * 1024 * 1024
 OWN_ROUTES = ("x", "x")
 OVER_ROUTES = ("y", "y")
-STEPS = "r0 r2 h0 h1 r1 r3 m0 m2 m1 m3"
-FIRST_STEPS = ""
+STEPS = ("r0", "r2", "h0", "h1", "r1", "r3", "m0", "m2", "m1", "m3")
 
 
 def swap_lane_groups(tiles):
@@ -54,8 +53,8 @@
     n_space, n_snap, total_cells,
     s_hbm, v_hbm, ev_hbm, h_hbm,
     modes_ref, coef_ref,
-    s_v, h_v, ev_ref, h_all, recv, staged, e_all, acc, pack, partner, paired, sums, c_out, c_in, d_out, d_in, f_in,
-    s_sem, h_sem, ev_sem, a_send, a_recv, own_sem, hy_send, hy_recv, hz_send, hz_first, hz_rest, g_send, g_first, g_rest,
+    s_v, h_v, v_v, ev_ref, h_all, recv, staged, e_all, acc, pack, partner, paired, sums, c_out, c_in, d_out, d_in, f_in,
+    s_sem, h_sem, v_sem, ev_sem, a_send, a_recv, own_sem, hy_send, hy_recv, hz_send, hz_first, hz_rest, g_send, g_first, g_rest,
     k_send, k_recv, r_send, r_recv, c_send, c_recv,
 ):
     q, p = lax.axis_index("space"), lax.axis_index("snap")
@@ -109,6 +108,8 @@
 
     ev_copy = pltpu.make_async_copy(ev_hbm, ev_ref, ev_sem)
     ev_copy.start()
+    v_copy = pltpu.make_async_copy(v_hbm, v_v, v_sem)
+    v_copy.start()
     own = []
     for t in range(2):
         target = lax.rem(row_y + t, 2) * n_far + line
@@ -122,8 +123,6 @@
         rows = pl.ds(m * ROW_TILE, ROW_TILE)
         return pltpu.make_async_copy(s_hbm.at[rows], s_v.at[rows], s_sem.at[m])
 
-    for m in range(tiles_m):
-        s_copy(m).start()
     row = lax.broadcasted_iota(jnp.int32, (SUBLANES, LANES), 0)
     ev_copy.wait()
     values = jnp.zeros((SUBLANES, LANES), jnp.float32)
@@ -135,6 +134,7 @@
     h_all[far] = h_v[...].astype(jnp.float32)
     for t in range(2):
         own[t].wait()
+    v_copy.wait()
     pl.semaphore_wait(barrier, n_snap - 1 + 2 * (n_space - 1))
 
     @pl.loop(1, n_far)
@@ -144,7 +144,7 @@
             target = lax.rem(row_y + t, 2) * n_far + other
             cols = pl.ds(pl.multiple_of(target * LANES, LANES), LANES)
             remote(
-                v_hbm.at[:, cols], recv.at[t, line], a_send, a_recv.at[line // groups], q, row_y * n_far + other
+                v_v.at[:, cols], recv.at[t, line], a_send, a_recv.at[line // groups], q, row_y * n_far + other
             ).start()
 
     remote(h_all.at[far], h_all.at[far], hy_send, hy_recv, q, facing * CORES + core).start()
@@ -274,7 +274,7 @@
                 drain(h_all.at[pl.ds(0, 3)], hz_rest.at[kind])
 
     def run(steps):
-        for name in steps.split():
+        for name in steps:
             at = int(name[1])
             if name[0] == "h":
                 relay_held(at)
@@ -294,10 +294,10 @@
         start_chunk(i)
         start_chunk(parts + i)
         if i == 0:
+            for m in range(tiles_m):
+                s_copy(m).start()
             drain(h_all.at[0], hy_recv)
             start_held(1)
-            if parts > 1:
-                run(FIRST_STEPS)
     run(STEPS)
 
     @pl.loop(0, tiles_m)
@@ -404,6 +404,7 @@
             scratch_shapes=[
                 vmem((cells, snaps), jnp.bfloat16),
                 vmem(held_out.shape, jnp.bfloat16),
+                vmem((SUBLANES, snaps), f32),
                 pltpu.SMEM((modes,), f32),
                 vmem((n_far, *held_out.shape), f32),
                 vmem((2, n_far, *tile), f32),
@@ -420,6 +421,7 @@
                 vmem((n_far, *tile), f32),
                 vmem((n_near, *tile), f32),
                 dma((cells // ROW_TILE,)),
+                dma,
                 dma,
                 dma,
                 dma,

time: 46.5 us -> 46.4 us (level)
  no operation moved by 1% of the time
where the time goes in v5:
time: 46.4 us; the launch traced here: 46.3 us
  Pallas kernels  45.6 us (98%)
  between operations  0.64 us (1%)
    pallas_call x1, Pallas kernels, per_device(): pl.pallas_call(functools.partial(kernel, n_space, n_snap, cells * n_space...  45 us

profile of v5, /device:TPU:1, one launch (start us, length us, event | category | flops | bytes accessed | tf_op | source)
XLA Modules:
  0.0 46.3 jit_solution(18241783214259256008)
XLA Ops:
  0.6 45.0 %shard_map.59 = (f32[16,128]{1,0:T(8,128)S(1)}, f32[16,8,128]{2,1,0:T(8,128)S(1)}) custom-call(bf16[1024,4096]{1,0:T(8,128)(2,1)} %s_hbm.1, f32[8,4096]{1,0:T(8,128)} %bitcast.1, f32[64]{0:T(128)} %ev_hbm.1, bf16[32,256]{1,0:T(8,128)(2,1)} %h_hbm.1), custom_call_target="tpu_custom_call" | custom-call | tf_op jit(solution)/shard_map/pallas_call | solution.py:394
  45.6 0.7 %shard_map.60 = (bf16[32,64]{1,0:T(8,128)(2,1)}, f32[64,256]{1,0:T(8,128)}) custom-call(f32[16,128]{1,0:T(8,128)S(1)} %get-tuple-element.4.total_ref, f32[16,8,128]{2,1,0:T(8,128)S(1)} %get-tuple-element.5.tiles_ref), custom_call_target="tpu_custom_call" | custom-call | tf_op jit(solution)/shard_map/pallas_call | solution.py:449

commit v6 on v5

--- a/solution.py
+++ b/solution.py
@@ -123,6 +123,19 @@
         rows = pl.ds(m * ROW_TILE, ROW_TILE)
         return pltpu.make_async_copy(s_hbm.at[rows], s_v.at[rows], s_sem.at[m])
 
+    v_copy.wait()
+    pl.semaphore_wait(barrier, n_snap - 1 + 2 * (n_space - 1))
+
+    @pl.loop(1, n_far)
+    def _(d):
+        other = lax.rem(line + d, n_far)
+        for t in range(2):
+            target = lax.rem(row_y + t, 2) * n_far + other
+            cols = pl.ds(pl.multiple_of(target * LANES, LANES), LANES)
+            remote(
+                v_v.at[:, cols], recv.at[t, line], a_send, a_recv.at[line // groups], q, row_y * n_far + other
+            ).start()
+
     row = lax.broadcasted_iota(jnp.int32, (SUBLANES, LANES), 0)
     ev_copy.wait()
     values = jnp.zeros((SUBLANES, LANES), jnp.float32)
@@ -134,18 +147,6 @@
     h_all[far] = h_v[...].astype(jnp.float32)
     for t in range(2):
         own[t].wait()
-    v_copy.wait()
-    pl.semaphore_wait(barrier, n_snap - 1 + 2 * (n_space - 1))
-
-    @pl.loop(1, n_far)
-    def _(d):
-        other = lax.rem(line + d, n_far)
-        for t in range(2):
-            target = lax.rem(row_y + t, 2) * n_far + other
-            cols = pl.ds(pl.multiple_of(target * LANES, LANES), LANES)
-            remote(
-                v_v.at[:, cols], recv.at[t, line], a_send, a_recv.at[line // groups], q, row_y * n_far + other
-            ).start()
 
     remote(h_all.at[far], h_all.at[far], hy_send, hy_recv, q, facing * CORES + core).start()
 

time: 46.4 us -> 46.4 us (level)
  no operation moved by 1% of the time
where the time goes in v6:
time: 46.4 us; the launch traced here: 46.3 us
  Pallas kernels  45.6 us (98%)
  between operations  0.64 us (1%)
    pallas_call x1, Pallas kernels, per_device(): pl.pallas_call(functools.partial(kernel, n_space, n_snap, cells * n_space...  45 us

profile of v6, /device:TPU:1, one launch (start us, length us, event | category | flops | bytes accessed | tf_op | source)
XLA Modules:
  0.0 46.3 jit_solution(16320469127218522019)
XLA Ops:
  0.6 45.0 %shard_map.59 = (f32[16,128]{1,0:T(8,128)S(1)}, f32[16,8,128]{2,1,0:T(8,128)S(1)}) custom-call(bf16[1024,4096]{1,0:T(8,128)(2,1)} %s_hbm.1, f32[8,4096]{1,0:T(8,128)} %bitcast.1, f32[64]{0:T(128)} %ev_hbm.1, bf16[32,256]{1,0:T(8,128)(2,1)} %h_hbm.1), custom_call_target="tpu_custom_call" | custom-call | tf_op jit(solution)/shard_map/pallas_call | solution.py:395
  45.6 0.7 %shard_map.60 = (bf16[32,64]{1,0:T(8,128)(2,1)}, f32[64,256]{1,0:T(8,128)}) custom-call(f32[16,128]{1,0:T(8,128)S(1)} %get-tuple-element.4.total_ref, f32[16,8,128]{2,1,0:T(8,128)S(1)} %get-tuple-element.5.tiles_ref), custom_call_target="tpu_custom_call" | custom-call | tf_op jit(solution)/shard_map/pallas_call | solution.py:450
